TPU v7x, 32 devices: a whole 2x2x4 slice. The times are simulated.
32 devices in a mesh: seg: 16 (over z, x, core), band: 2 (over y).
Axes of the slice: x: 2, y: 2, z: 4, core: 2. Of those that a mesh axis runs over, the one named last changes fastest.
Arguments:
- spectra: bfloat16 [2, 16384, 1024], P(None, 'seg', 'band'), may hold values from -100 to 100, as said below
- pair_first: int32 [65536], P('seg'), may hold values from 0 to 16383, as said below
- pair_second: int32 [65536], P('seg'), may hold values from 0 to 16383, as said below
- pair_bin: int32 [65536], P('seg'), may hold values from 0 to 127, as said below
Outputs:
- correlation_stack: float32 [128, 1024], P('seg', 'band')
Inputs may be any that keep to these rules, and one draw needn't show every extreme that they name: The spectra are finite; their magnitude varies from channel to channel and from bin to bin. `pair_first`: rows s * 4096 to (s + 1) * 4096 - 1 name channels of segment s, that is s * 1024 to (s + 1) * 1024 - 1. pair_second differs from pair_first of the same row by 1 to 256 in either direction; some row of every segment differs by exactly 256. `pair_bin`: offset bins s * 8 to (s + 1) * 8 - 1 belong to segment s; of one segment's rows at most 256 have bins of any one segment, and in every draw the bins of some segment receive exactly 256 rows from every segment.
All inputs are finite; a program needn't handle non-finite values.
Results may differ from a plain program's by a relative error of at most 0.0054.
Values may be sent and summed in bfloat16 or wider, within the bound.
A program may use at most 64 MiB of HBM per device.

v0:
```python
import math

import jax
import jax.numpy as jnp
from jax import lax
from jax.sharding import PartitionSpec as P

OB_DEV = 8
REACH = 256
FREQ = 1024
LAGS = 1024
HALF_WIN = 64
CAP = 256


epsilon = 1e-06


def extended(block, sides, width):
    for axis, dim in sides:
        count = lax.axis_size(axis)
        forward = [(i, i + 1) for i in range(count - 1)]
        backward = [(target, source) for source, target in forward]
        low = lax.ppermute(
            lax.slice_in_dim(block, block.shape[dim] - width, None, axis=dim), axis, forward
        )
        high = lax.ppermute(lax.slice_in_dim(block, 0, width, axis=dim), axis, backward)
        block = jnp.concatenate([low, block, high], axis=dim)
    return block


def window_matrix(local_bins, half_width):
    padded_index = jnp.arange(local_bins + 2 * half_width)[:, None]
    bin_index = jnp.arange(local_bins)[None, :]
    inside = (padded_index >= bin_index) & (padded_index <= bin_index + 2 * half_width)
    return inside.astype(jnp.float32)


def lag_table(first_bin, local_bins, total_bins, lag_count):
    frequency = first_bin + jnp.arange(local_bins, dtype=jnp.int32)
    lag_index = jnp.arange(lag_count, dtype=jnp.int32) - lag_count // 2
    residue = frequency[:, None] * lag_index[None, :] % (2 * total_bins)
    angles = residue.astype(jnp.float32) * (math.pi / total_bins)
    cosine = jnp.cos(angles) / total_bins
    negsine = -jnp.sin(angles) / total_bins
    return jnp.concatenate([cosine, negsine], axis=0).astype(jnp.bfloat16)


def per_device(spectra, pair_first, pair_second, pair_bin):
    seg_position = lax.axis_index("seg")
    band_position = lax.axis_index("band")
    segments = lax.axis_size("seg")
    channels = spectra.shape[1]
    local_bins = spectra.shape[2]
    real_part = spectra[0].astype(jnp.float32)
    imag_part = spectra[1].astype(jnp.float32)
    power_sum = real_part * real_part + imag_part * imag_part
    padded_power = extended(power_sum, (("band", 1),), HALF_WIN)
    window_sum = jnp.dot(
        padded_power, window_matrix(local_bins, HALF_WIN), precision=lax.Precision.HIGHEST
    )
    scaling = lax.rsqrt(window_sum / (2 * HALF_WIN + 1) + epsilon)
    whitened = jnp.concatenate([real_part * scaling, imag_part * scaling], axis=1).astype(
        jnp.bfloat16
    )
    first_rows = whitened[pair_first - seg_position * channels]
    near_rows = extended(whitened, (("seg", 0),), REACH)
    second_rows = near_rows[pair_second - seg_position * channels + REACH]
    first_real = first_rows[:, :local_bins].astype(jnp.float32)
    first_imag = first_rows[:, local_bins:].astype(jnp.float32)
    second_real = second_rows[:, :local_bins].astype(jnp.float32)
    second_imag = second_rows[:, local_bins:].astype(jnp.float32)
    cross_real = first_real * second_real + first_imag * second_imag
    cross_imag = first_imag * second_real - first_real * second_imag
    cross_both = jnp.concatenate([cross_real, cross_imag], axis=1).astype(jnp.bfloat16)
    table = lag_table(band_position * local_bins, local_bins, FREQ, LAGS)
    owner_seg = pair_bin // OB_DEV
    owner_hits = (owner_seg[:, None] == jnp.arange(segments, dtype=jnp.int32)[None, :]).astype(
        jnp.int32
    )
    earlier_hits = jnp.cumsum(owner_hits, axis=0) - owner_hits
    slot_rank = jnp.sum(earlier_hits * owner_hits, axis=1)
    slot_index = owner_seg * CAP + slot_rank
    send_rows = (
        jnp.zeros((segments * CAP, 2 * local_bins), jnp.bfloat16).at[slot_index].set(cross_both)
    )
    send_tags = jnp.zeros((segments * CAP,), jnp.int32).at[slot_index].set(pair_bin % OB_DEV + 1)
    recv_rows, recv_tags = (
        lax.all_to_all(
            send_rows.reshape(segments, CAP, 2 * local_bins),
            "seg",
            split_axis=0,
            concat_axis=0,
            tiled=True,
        ),
        lax.all_to_all(
            send_tags.reshape(segments, CAP), "seg", split_axis=0, concat_axis=0, tiled=True
        ),
    )
    group_size = math.gcd(segments, max(1, 512 // CAP))
    block_rows = recv_rows.reshape(segments // group_size, group_size * CAP, 2 * local_bins)
    block_tags = recv_tags.reshape(segments // group_size, group_size * CAP)
    bin_labels = jnp.arange(1, OB_DEV + 1, dtype=jnp.int32)

    def stack_block(running, block_data):
        slot_rows, slot_tags = block_data
        slot_lags = jnp.dot(slot_rows, table, preferred_element_type=jnp.float32)
        member_table = (slot_tags[:, None] == bin_labels[None, :]).astype(jnp.float32)
        added = lax.dot_general(
            member_table, slot_lags, (((0,), (0,)), ((), ())), precision=lax.Precision.HIGHEST
        )
        return (running + added, None)

    partial_lags, _ = lax.scan(
        stack_block, jnp.zeros((OB_DEV, LAGS), jnp.float32), (block_rows, block_tags)
    )
    return lax.psum_scatter(partial_lags, "band", scatter_dimension=1, tiled=True)


def solution(mesh):
    placed = (P(None, "seg", "band"), P("seg"), P("seg"), P("seg"))
    return jax.shard_map(
        per_device, mesh=mesh, in_specs=placed, out_specs=P("seg", "band"), check_vma=False
    )
```

profile of v0, /device:TPU:0, one launch (start us, length us, event | category | flops | bytes accessed | tf_op | source)
XLA Modules:
  0.0 380.2 jit_solution(5264111985207984895)
XLA Ops:
  6.5 1.7 fusion.48
  8.2 0.5 copy.17
  8.8 0.5 copy.18
  9.3 0.0 copy-start.1
  9.3 0.0 copy-start.4
  9.3 0.4 fusion.24
  9.7 0.0 copy-start.2
  9.8 0.5 copy-done.1
  10.3 0.8 copy-done.2
  11.1 4.9 %collective-permute-start = (f32[1024,64]{0,1:T(8,128)S(1)}, f32[1024,64]{0,1:T(8,128)S(1)}, u32[]{:S(2)}, u32[]{:S(2)}) collective-permute-start(f32[1024,64]{0,1:T(8,128)S(1)} %get-tuple-element.74), channel_id=1, source_target_pairs={{0,1},{2,3},{4,5},{6,7},{8,9},{10,11},{12,13},{14,15},{16,17},{18,... | collective-permute-start | bytes 786440 | tf_op jit(solution)/shard_map/ppermute | solution.py:24
  16.0 1.3 collective-permute-start.1
  17.3 0.0 copy-done.4
  17.3 4.6 %reduce-window.6 = s32[16,32,128]{2,1,0:T(8,128)S(1)} reduce-window(s32[16,32,128]{2,1,0:T(8,128)S(1)} %fusion.38, s32[]{:T(128)} %constant.76.clone.1), window={size=1x1x128 pad=0_0x0_0x127_0}, to_apply=%region_0.1 | reduce-window | flops 8323072 | bytes 524292 | tf_op jit(solution)/shard_map/reduce-window
  22.0 0.5 slice_reduce_fusion
  22.4 0.2 reduce-window.9
  22.6 0.1 broadcast_add_fusion
  22.8 0.2 fusion.37
  23.0 0.0 collective-permute-done
  23.0 2.8 collective-permute-done.1
  25.7 5.0 %fusion.26 = (bf16[1024,512]{0,1:T(8,128)(2,1)S(1)}, bf16[1024,512]{0,1:T(8,128)(2,1)S(1)}) fusion(bf16[1,1024,512]{1,2,0:T(8,128)(2,1)} %copy-done.1, bf16[1,1024,512]{1,2,0:T(8,128)(2,1)S(1)} %copy.17, s32[512]{0:T(512)S(1)} %iota_add_fusion.3, f32[1024,64]{0,1:T(8,128)} %collective-permute-done.1, f32[1024,512]{0,1:T(8,128)} %copy-done.2, ...), kind=kOutput, calls=%fused_computation.51 | convolution fusion | flops 4033019904 | bytes 6817792 | tf_op jit(solution)/shard_map/dot_general | solution.py:59
  30.8 0.0 copy-start
  30.8 0.0 copy-start.5
  30.8 0.0 copy-start.6
  30.8 1.1 fusion.33
  31.9 2.1 collective-permute-start.2
  34.0 1.3 collective-permute-start.3
  35.3 16.1 %scatter_custom_fusion = s32[4096]{0:T(1024)} fusion(s32[4096]{0:T(1024)S(1)} %compare_select_fusion.2, s32[4096]{0:T(1024)S(1)} %get-tuple-element.78, s32[]{:T(128)} %constant.76.clone.1), kind=kCustom, calls=%fused_computation.88 | custom fusion | bytes 16388 | tf_op jit(solution)/shard_map/scatter | solution.py:87
  51.4 8.1 %all-to-all-start = ((s32[16,1,256]{2,1,0:T(1,128)}), s32[16,1,256]{2,1,0:T(1,128)S(1)}, u32[]{:S(2)}, u32[]{:S(2)}) async-start(s32[16,1,256]{2,1,0:T(1,128)} %bitcast.2), calls=%async_computation | async-start | bytes 32768 | tf_op jit(solution)/shard_map/all_to_all | solution.py:96
  59.6 1.5 pad_maximum_fusion.1
  61.1 2.9 copy.15
  63.9 18.2 %gather_fusion = bf16[4096,1024]{1,0:T(8,128)(2,1)} fusion(bf16[1024,1024]{1,0:T(8,128)(2,1)S(1)} %copy.15, s32[4096]{0:T(1024)S(1)} %get-tuple-element.82), kind=kCustom, calls=%fused_computation | custom fusion | bytes 16793600 | tf_op jit(solution)/shard_map/gather | solution.py:66
  82.1 0.0 collective-permute-done.2
  82.1 0.0 collective-permute-done.3
  82.1 5.5 %pad_maximum_fusion = bf16[1536,1024]{0,1:T(8,128)(2,1)} fusion(bf16[256,1024]{0,1:T(8,128)(2,1)} %collective-permute-done.3, bf16[1024,512]{0,1:T(8,128)(2,1)S(1)} %get-tuple-element.72, bf16[1024,512]{0,1:T(8,128)(2,1)} %copy-done, bf16[256,1024]{0,1:T(8,128)(2,1)} %collective-permute-done.2), kind=kLoop, calls=%fused_computation.31 | loop fusion | flops 12582912 | bytes 6291456 | tf_op jit(solution)/shard_map/concatenate | solution.py:28
  87.7 3.2 copy.16
  90.9 18.2 %gather_fusion.1 = bf16[4096,1024]{1,0:T(8,128)(2,1)} fusion(bf16[1536,1024]{1,0:T(8,128)(2,1)S(1)} %copy.16, s32[4096]{0:T(1024)S(1)} %get-tuple-element.83), kind=kCustom, calls=%fused_computation.1 | custom fusion | bytes 16793600 | tf_op jit(solution)/shard_map/gather | solution.py:68
  109.1 9.3 %fusion.10 = (bf16[4096,512]{1,0:T(8,128)(2,1)}, bf16[4096,512]{1,0:T(8,128)(2,1)}) fusion(bf16[4096,1024]{1,0:T(8,128)(2,1)} %gather_fusion.1, bf16[4096,1024]{1,0:T(8,128)(2,1)} %gather_fusion), kind=kLoop, calls=%fused_computation.20 | loop fusion | flops 25165824 | bytes 25165824 | tf_op jit(solution)/shard_map/convert.4
  118.4 24.2 %scatter_custom_fusion.1 = bf16[4096,1024]{1,0:T(8,128)(2,1)} fusion(s32[4096]{0:T(1024)S(1)} %compare_select_fusion.2, bf16[4096,512]{1,0:T(8,128)(2,1)} %get-tuple-element.69, bf16[]{:T(256)} %constant.101, bf16[4096,512]{1,0:T(8,128)(2,1)} %get-tuple-element.68, bf16[]{:T(256)} %constant.78.clone.1), kind=kCustom, calls=%fused_computation.23 | custom fusion | flops 16777216 | bytes 16777220 | tf_op jit(solution)/shard_map/scatter | solution.py:85
  142.6 0.0 all-to-all-done
  142.6 6.0 %all-to-all-start.1 = ((bf16[16,256,1024]{2,1,0:T(8,128)(2,1)}), bf16[16,256,1024]{2,1,0:T(8,128)(2,1)}, u32[]{:S(2)}, u32[]{:S(2)}) async-start(bf16[16,256,1024]{2,1,0:T(8,128)(2,1)} %bitcast.44), calls=%async_computation.1 | async-start | bytes 16777216 | tf_op jit(solution)/shard_map/all_to_all | solution.py:89
  148.6 0.3 reduce-scatter.2.cloned.1.call-start
  149.0 9.1 %multiply_convert_fusion.1 = (bf16[512,1024]{1,0:T(8,128)(2,1)S(1)}, bf16[512,1024]{1,0:T(8,128)(2,1)S(1)}) fusion(s32[1024]{0:T(1024)S(1)} %iota_add_fusion.1, s32[512]{0:T(512)S(1)} %iota_add_fusion.2), kind=kLoop, calls=%fused_computation.57 | loop fusion | flops 9961472 | bytes 2103296 | tf_op jit(solution)/shard_map/convert.2
  158.1 1.5 pad_maximum_fusion.2
  159.6 139.7 %all-to-all-done.1 = bf16[16,256,1024]{2,1,0:T(8,128)(2,1)} async-done(((bf16[16,256,1024]{2,1,0:T(8,128)(2,1)}), bf16[16,256,1024]{2,1,0:T(8,128)(2,1)}, u32[]{:S(2)}, u32[]{:S(2)}) %all-to-all-start.1) | async-done | bytes 8388640 | tf_op jit(solution)/shard_map/all_to_all | solution.py:89
  299.4 32.5 %while.11 = (s32[]{:T(128)}, f32[8,1024]{1,0:T(8,128)S(1)}, s32[8,512]{1,0:T(8,128)S(1)}, bf16[8,512,1024]{2,1,0:T(8,128)(2,1)}, bf16[1024,1024]{1,0:T(8,128)(2,1)}, /*index=5*/s32[]{:T(128)}, s32[]{:T(128)}) while((s32[]{:T(128)}, f32[8,1024]{1,0:T(8,128)S(1)}, s32[8,512]{1,0:T(8,128)S(1)}, bf16[8,512,1024]{2,1,0:T(8,128)(2,1)}, ...), condition=%wide.region_6.7_spmd.clone, body=%wide.region_5.6_spmd.clone.sunk | while | flops 1124093952 | bytes 7412379 | solution.py:114
  299.4 3.2 fusion.60
  302.6 0.9 convolution_add_fusion.2
  303.4 3.2 fusion.60
  306.6 0.9 convolution_add_fusion.2
  307.5 3.2 fusion.60
  310.7 0.9 convolution_add_fusion.2
  311.6 3.2 fusion.60
  314.8 0.9 convolution_add_fusion.2
  315.6 3.2 fusion.60
  318.8 0.9 convolution_add_fusion.2
  319.7 3.2 fusion.60
  322.9 0.9 convolution_add_fusion.2
  323.8 3.2 fusion.60
  327.0 0.9 convolution_add_fusion.2
  327.8 3.2 fusion.60
  331.0 0.9 convolution_add_fusion.2
  331.9 0.6 copy-done.3
  332.5 0.0 reduce-scatter.2.cloned.1.call-update
  332.5 40.9 %reduce-scatter.2.cloned.1.call-done = f32[8,512]{1,0:T(8,128)} async-done(((f32[8,1024]{1,0:T(8,128)}), f32[8,512]{1,0:T(8,128)}) %reduce-scatter.2.cloned.1.call-update) | async-done | bytes 16400 | tf_op jit(solution)/shard_map/reduce_scatter | solution.py:117
  (31 shorter events, 0.3 us)
Async XLA Ops:
  9.3 1.0 copy-start.1
  9.3 8.0 %copy-start.4 = (s32[4096]{0:T(1024)S(1)}, s32[4096]{0:T(1024)}, u32[]{:S(2)}) copy-start(s32[4096]{0:T(1024)} %param.9) | copy-start | bytes 49156
  9.7 1.3 copy-start.2
  11.1 11.9 %collective-permute-start = (f32[1024,64]{0,1:T(8,128)S(1)}, f32[1024,64]{0,1:T(8,128)S(1)}, u32[]{:S(2)}, u32[]{:S(2)}) collective-permute-start(f32[1024,64]{0,1:T(8,128)S(1)} %get-tuple-element.74), channel_id=1, source_target_pairs={{0,1},{2,3},{4,5},{6,7},{8,9},{10,11},{12,13},{14,15},{16,17},{18,... | collective-permute-start | bytes 786440 | tf_op jit(solution)/shard_map/ppermute | solution.py:24
  16.0 9.8 %collective-permute-start.1 = (f32[1024,64]{0,1:T(8,128)S(1)}, f32[1024,64]{0,1:T(8,128)}, u32[]{:S(2)}, u32[]{:S(2)}) collective-permute-start(f32[1024,64]{0,1:T(8,128)S(1)} %get-tuple-element.75), channel_id=1, source_target_pairs={{1,0},{3,2},{5,4},{7,6},{9,8},{11,10},{13,12},{15,14},{17,16},{19,... | collective-permute-start | bytes 786440 | tf_op jit(solution)/shard_map/ppermute | solution.py:27
  30.8 28.8 %copy-start = (bf16[1024,512]{0,1:T(8,128)(2,1)}, bf16[1024,512]{0,1:T(8,128)(2,1)S(1)}, u32[]{:S(2)}) copy-start(bf16[1024,512]{0,1:T(8,128)(2,1)S(1)} %get-tuple-element.73) | copy-start | bytes 3145732
  30.8 28.7 %copy-start.5 = (s32[4096]{0:T(1024)S(1)}, s32[4096]{0:T(1024)}, u32[]{:S(2)}) copy-start(s32[4096]{0:T(1024)} %param.7) | copy-start | bytes 49156
  30.8 28.7 %copy-start.6 = (s32[4096]{0:T(1024)S(1)}, s32[4096]{0:T(1024)}, u32[]{:S(2)}) copy-start(s32[4096]{0:T(1024)} %param.8) | copy-start | bytes 49156
  31.9 50.2 %collective-permute-start.2 = (bf16[256,1024]{0,1:T(8,128)(2,1)}, bf16[256,1024]{0,1:T(8,128)(2,1)}, u32[]{:S(2)}, u32[]{:S(2)}) collective-permute-start(bf16[256,1024]{0,1:T(8,128)(2,1)} %get-tuple-element.70), channel_id=1, source_target_pairs={{0,2},{2,4},{4,6},{6,8},{8,10},{10,12},{12,14},{14,16},{16,18},{18... | collective-permute-start | bytes 1572872 | tf_op jit(solution)/shard_map/ppermute | solution.py:24
  34.0 48.1 %collective-permute-start.3 = (bf16[256,1024]{0,1:T(8,128)(2,1)}, bf16[256,1024]{0,1:T(8,128)(2,1)}, u32[]{:S(2)}, u32[]{:S(2)}) collective-permute-start(bf16[256,1024]{0,1:T(8,128)(2,1)} %get-tuple-element.71), channel_id=1, source_target_pairs={{2,0},{4,2},{6,4},{8,6},{10,8},{12,10},{14,12},{16,14},{18,16},{20... | collective-permute-start | bytes 1572872 | tf_op jit(solution)/shard_map/ppermute | solution.py:27
  51.4 91.2 %all-to-all-start = ((s32[16,1,256]{2,1,0:T(1,128)}), s32[16,1,256]{2,1,0:T(1,128)S(1)}, u32[]{:S(2)}, u32[]{:S(2)}) async-start(s32[16,1,256]{2,1,0:T(1,128)} %bitcast.2), calls=%async_computation | async-start | bytes 32768 | tf_op jit(solution)/shard_map/all_to_all | solution.py:96
  142.6 156.8 %all-to-all-start.1 = ((bf16[16,256,1024]{2,1,0:T(8,128)(2,1)}), bf16[16,256,1024]{2,1,0:T(8,128)(2,1)}, u32[]{:S(2)}, u32[]{:S(2)}) async-start(bf16[16,256,1024]{2,1,0:T(8,128)(2,1)} %bitcast.44), calls=%async_computation.1 | async-start | bytes 16777216 | tf_op jit(solution)/shard_map/all_to_all | solution.py:89
  148.6 224.7 %reduce-scatter.2.cloned.1.call-start = ((), (), s32[]{:S(2)}) async-start(), calls=%async_computation.3 | async-start | bytes 49152 | tf_op jit(solution)/shard_map/reduce_scatter | solution.py:117
  331.9 0.6 copy-start.3
Sparse Core Ops, SparseCore 0:
  332.7 40.6 reduce-scatter.1
where the time goes:
time: 381 us; the launch traced here: 380 us
  waiting for transfers between devices  183 us (48%)
  local copies, waits for them, and re-layouts  63.8 us (17%)
  other arithmetic  58 us (15%)
  matrix products  37.3 us (10%)
  starting transfers between devices  24 us (6%)
  between operations  13.7 us (4%)
    all_to_all x1, waiting for transfers between devices, per_device(): lax.all_to_all(send_rows.reshape(segments, CAP, 2 * local_bins), 'seg', s...  140 us
    reduce_scatter x1, waiting for transfers between devices, per_device(): lax.psum_scatter(partial_lags, 'band', scatter_dimension=1, tiled=True)  40.9 us
    dot_general x8, matrix products, stack_block(): slot_lags = jnp.dot(slot_rows, table, preferred_element_type=jnp.float32)  25.4 us
    scatter x1, other arithmetic, per_device(): jnp.zeros((segments * CAP, 2 * local_bins), jnp.bfloat16).at[slot_index]  24.2 us
    another operation x5, other arithmetic  23.4 us
    gather x1, local copies, waits for them, and re-layouts, per_device(): second_rows = near_rows[pair_second - seg_position * channels + REACH]  18.2 us
    gather x1, local copies, waits for them, and re-layouts, per_device(): first_rows = whitened[pair_first - seg_position * channels]  18.2 us
    scatter x1, local copies, waits for them, and re-layouts, per_device(): jnp.zeros((segments * CAP,), jnp.int32).at[slot_index]  16.1 us
  transfers between devices with their start and end apart: 7, of which 3 were waited for; matrix products, arithmetic and copies ran while one was open for 30% of the time, Pallas kernels for 0%

commit v1 on v0

v1 whole, which is shorter than its diff:
```python
import functools
import math

import jax
import jax.numpy as jnp
from jax import lax
from jax.experimental import pallas as pl
from jax.experimental.pallas import tpu as pltpu
from jax.sharding import PartitionSpec as P

OB_DEV = 8
REACH = 256
FREQ = 1024
LAGS = 1024
HALF_WIN = 64
BANKS = 4
LANES = 128
FINE = 32
NEAR_SEGS = 4
MESH = pl.DeviceIdType.MESH

epsilon = 1e-06


def extended(block, sides, width):
    for axis, dim in sides:
        count = lax.axis_size(axis)
        forward = [(i, i + 1) for i in range(count - 1)]
        backward = [(target, source) for source, target in forward]
        low = lax.ppermute(
            lax.slice_in_dim(block, block.shape[dim] - width, None, axis=dim), axis, forward
        )
        high = lax.ppermute(lax.slice_in_dim(block, 0, width, axis=dim), axis, backward)
        block = jnp.concatenate([low, block, high], axis=dim)
    return block


def window_matrix(local_bins, half_width):
    padded_index = jnp.arange(local_bins + 2 * half_width)[:, None]
    bin_index = jnp.arange(local_bins)[None, :]
    inside = (padded_index >= bin_index) & (padded_index <= bin_index + 2 * half_width)
    return inside.astype(jnp.float32)


def circle(first, step, count):
    rows = lax.broadcasted_iota(jnp.int32, (count, LAGS), 0) * step + first
    lags = lax.broadcasted_iota(jnp.int32, (count, LAGS), 1) - LAGS // 2
    residue = jnp.bitwise_and(rows * lags, 2 * FREQ - 1)
    residue = residue - jnp.where(residue >= FREQ, 2 * FREQ, 0)
    angles = residue.astype(jnp.float32) * (math.pi / FREQ)
    return jnp.cos(angles), jnp.sin(angles)


def write_basis(first_bin, local_bins, table):
    coarse_cos, coarse_sin = circle(first_bin, FINE, local_bins // FINE)
    fine_cos, fine_sin = circle(0, 1, FINE)
    fine_cos, fine_sin = fine_cos * (1.0 / FREQ), fine_sin * (1.0 / FREQ)
    for i in range(local_bins // FINE):
        cc, cs = coarse_cos[i : i + 1], coarse_sin[i : i + 1]
        table[i * FINE : (i + 1) * FINE, :] = (cc * fine_cos - cs * fine_sin).astype(jnp.bfloat16)
        table[local_bins + i * FINE : local_bins + (i + 1) * FINE, :] = (
            -(cs * fine_cos + cc * fine_sin)
        ).astype(jnp.bfloat16)


def pair_kernel(
    local_bins, bins, first_ref, second_ref, bin_ref, white_ref, out_ref, rows, table, *banks
):
    parts = 2 * local_bins // LANES
    half = parts // 2
    channels = white_ref.shape[0]
    write_basis(lax.axis_index("band") * local_bins, local_bins, table)
    for bank in banks:
        bank[...] = jnp.zeros_like(bank)
    for j in range(parts):
        rows[pl.ds(j, channels, stride=parts), :] = white_ref[
            :, j * LANES : (j + 1) * LANES
        ].astype(jnp.float32)

    def group(step, carry):
        base = step * BANKS
        updates = []
        for k, bank in enumerate(banks):
            a = pl.multiple_of(first_ref[base + k], parts)
            b = pl.multiple_of(second_ref[base + k], parts)
            o = pl.multiple_of(bin_ref[base + k], 2 * parts)
            first = rows[pl.ds(a, parts), :]
            second = rows[pl.ds(b, parts), :]
            straight = bank[pl.ds(o, parts), :] + first * second
            crossed = bank[pl.ds(o + parts, parts), :] + pltpu.roll(first, half, 0) * second
            updates.append((bank, o, straight, crossed))
        for bank, o, straight, crossed in updates:
            bank[pl.ds(o, parts), :] = straight
            bank[pl.ds(o + parts, parts), :] = crossed
        return carry

    lax.fori_loop(0, first_ref.shape[0] // BANKS, group, 0, unroll=4)

    def stacked(j):
        total = banks[0][pl.ds(j, bins, stride=2 * parts), :]
        for bank in banks[1:]:
            total = total + bank[pl.ds(j, bins, stride=2 * parts), :]
        return total

    lags = jnp.zeros((bins, LAGS), jnp.float32)
    for j in range(parts):
        if j < half:
            piece = stacked(j) + stacked(half + j)
        else:
            piece = stacked(parts + j - half) - stacked(parts + j)
        high = piece.astype(jnp.bfloat16)
        low = (piece - high.astype(jnp.float32)).astype(jnp.bfloat16)
        basis = table[j * LANES : (j + 1) * LANES, :]
        lags += jnp.dot(high, basis, preferred_element_type=jnp.float32)
        lags += jnp.dot(low, basis, preferred_element_type=jnp.float32)
    out_ref[...] = lags


def sum_kernel(segments, bands, lags_ref, out_ref, send, near, mid, far, s1, r1, s2, r2):
    near_count = NEAR_SEGS * bands
    far_count = segments // NEAR_SEGS
    width = LAGS // bands
    seg, band = lax.axis_index("seg"), lax.axis_index("band")
    row, col = seg // NEAR_SEGS, seg % NEAR_SEGS
    me = col * bands + band

    def near_peer(d):
        p = lax.rem(me + d, near_count)
        return p, (row * NEAR_SEGS + p // bands, lax.rem(p, bands))

    def far_peer(d):
        p = lax.rem(row + d, far_count)
        return p, (p * NEAR_SEGS + col, band)

    barrier = pltpu.get_barrier_semaphore()
    for d in range(1, near_count):
        pl.semaphore_signal(barrier, inc=1, device_id=near_peer(d)[1], device_id_type=MESH)
    for d in range(1, far_count):
        pl.semaphore_signal(barrier, inc=1, device_id=far_peer(d)[1], device_id_type=MESH)
    for p in range(near_count):
        c, b = p // bands, p % bands
        block = [
            lags_ref[
                (r * NEAR_SEGS + c) * OB_DEV : (r * NEAR_SEGS + c + 1) * OB_DEV,
                b * width : (b + 1) * width,
            ]
            for r in range(far_count)
        ]
        send[p] = jnp.concatenate(block, axis=0).astype(jnp.bfloat16)
    pl.semaphore_wait(barrier, near_count - 1 + far_count - 1)

    def near_copy(d):
        p, device = near_peer(d)
        return pltpu.make_async_remote_copy(
            src_ref=send.at[p], dst_ref=near.at[d], send_sem=s1.at[d], recv_sem=r1.at[d],
            device_id=device, device_id_type=MESH,
        )

    def far_copy(d):
        p, device = far_peer(d)
        return pltpu.make_async_remote_copy(
            src_ref=mid.at[p], dst_ref=far.at[d], send_sem=s2.at[d], recv_sem=r2.at[d],
            device_id=device, device_id_type=MESH,
        )

    for d in range(1, near_count):
        near_copy(d).start()
    total = send[me].astype(jnp.float32)
    for d in range(1, near_count):
        near_copy(d).wait_recv()
        total += near[d].astype(jnp.float32)
    for r in range(far_count):
        mid[r] = total[r * OB_DEV : (r + 1) * OB_DEV]
    for d in range(1, far_count):
        far_copy(d).start()
    result = mid[row]
    for d in range(1, far_count):
        far_copy(d).wait_recv()
        result += far[d]
    out_ref[...] = result
    for d in range(1, near_count):
        near_copy(d).wait_send()
    for d in range(1, far_count):
        far_copy(d).wait_send()


def stack_pairs(white, first, second, bins_at, local_bins, bins):
    parts = 2 * local_bins // LANES
    smem = pl.BlockSpec(memory_space=pltpu.SMEM)
    vmem = pl.BlockSpec(memory_space=pltpu.VMEM)
    return pl.pallas_call(
        functools.partial(pair_kernel, local_bins, bins),
        out_shape=jax.ShapeDtypeStruct((bins, LAGS), jnp.float32),
        in_specs=[smem, smem, smem, vmem],
        out_specs=vmem,
        scratch_shapes=[
            pltpu.VMEM((white.shape[0] * parts, LANES), jnp.float32),
            pltpu.VMEM((2 * local_bins, LAGS), jnp.bfloat16),
        ]
        + [pltpu.VMEM((bins * 2 * parts, LANES), jnp.float32)] * BANKS,
        compiler_params=pltpu.CompilerParams(vmem_limit_bytes=48 * 2**20),
        name="pairs",
    )(first, second, bins_at, white)


def sum_lags(lags, segments, bands):
    near_count, far_count = NEAR_SEGS * bands, segments // NEAR_SEGS
    width = LAGS // bands
    vmem = pl.BlockSpec(memory_space=pltpu.VMEM)
    dma = pltpu.SemaphoreType.DMA
    return pl.pallas_call(
        functools.partial(sum_kernel, segments, bands),
        out_shape=jax.ShapeDtypeStruct((OB_DEV, width), jnp.float32),
        in_specs=[vmem],
        out_specs=vmem,
        scratch_shapes=[
            pltpu.VMEM((near_count, far_count * OB_DEV, width), jnp.bfloat16),
            pltpu.VMEM((near_count, far_count * OB_DEV, width), jnp.bfloat16),
            pltpu.VMEM((far_count, OB_DEV, width), jnp.float32),
            pltpu.VMEM((far_count, OB_DEV, width), jnp.float32),
            dma((near_count,)), dma((near_count,)), dma((far_count,)), dma((far_count,)),
        ],
        compiler_params=pltpu.CompilerParams(
            collective_id=1, has_side_effects=True, vmem_limit_bytes=32 * 2**20
        ),
        name="sums",
    )(lags)


def per_device(spectra, pair_first, pair_second, pair_bin):
    seg_position = lax.axis_index("seg")
    segments = lax.axis_size("seg")
    bands = lax.axis_size("band")
    channels = spectra.shape[1]
    local_bins = spectra.shape[2]
    parts = 2 * local_bins // LANES
    real_part = spectra[0].astype(jnp.float32)
    imag_part = spectra[1].astype(jnp.float32)
    power_sum = real_part * real_part + imag_part * imag_part
    padded_power = extended(power_sum, (("band", 1),), HALF_WIN)
    window_sum = jnp.dot(
        padded_power, window_matrix(local_bins, HALF_WIN), precision=lax.Precision.HIGHEST
    )
    scaling = lax.rsqrt(window_sum / (2 * HALF_WIN + 1) + epsilon)
    whitened = jnp.concatenate([real_part * scaling, imag_part * scaling], axis=1).astype(
        jnp.bfloat16
    )
    near_rows = extended(whitened, (("seg", 0),), REACH)
    shift = REACH - seg_position * channels
    lags = stack_pairs(
        near_rows,
        (pair_first + shift) * parts,
        (pair_second + shift) * parts,
        pair_bin * (2 * parts),
        local_bins,
        segments * OB_DEV,
    )
    return sum_lags(lags, segments, bands)


def solution(mesh):
    placed = (P(None, "seg", "band"), P("seg"), P("seg"), P("seg"))
    return jax.shard_map(
        per_device, mesh=mesh, in_specs=placed, out_specs=P("seg", "band"), check_vma=False
    )
```

time: 381 us -> 78.2 us (0.21)
  waiting for transfers between devices: 183 us -> 18.1 us
  local copies, waits for them, and re-layouts: 63.8 us -> 0.83 us
  other arithmetic: 58 us -> 9.44 us
  Pallas kernels: 0 us -> 37.3 us
  matrix products: 37.3 us -> 3.1 us
  starting transfers between devices: 24 us -> 9.11 us
  between operations: 13.7 us -> 0.16 us
    all_to_all x2 -> x0, waiting for transfers between devices: 140 us -> none  [the longest x1 140 us: per_device(): lax.all_to_all(send_rows.reshape(segments, CAP, 2 * local_bins), 'seg', s...]
    reduce_scatter x1 -> x0, waiting for transfers between devices: 40.9 us -> none  [per_device(): lax.psum_scatter(partial_lags, 'band', scatter_dimension=1, tiled=True)]
    pallas_call x0 -> x2, Pallas kernels: none -> 37.3 us  [the longest x1 21.1 us: sum_lags(): pl.pallas_call(functools.partial(sum_kernel, segments, bands), out_shape=...]
    gather x2 -> x0, local copies, waits for them, and re-layouts: 36.4 us -> none  [the longest x1 18.2 us: per_device(): second_rows = near_rows[pair_second - seg_position * channels + REACH]]
    dot_general x16 -> x0, matrix products: 32.2 us -> none  [the longest x8 25.4 us: stack_block(): slot_lags = jnp.dot(slot_rows, table, preferred_element_type=jnp.float32)]
    scatter x1 -> x0, other arithmetic: 24.2 us -> none  [per_device(): jnp.zeros((segments * CAP, 2 * local_bins), jnp.bfloat16).at[slot_index]]
    another operation x5 -> x0, other arithmetic: 23.4 us -> none
    scatter x1 -> x0, local copies, waits for them, and re-layouts: 16.1 us -> none  [per_device(): jnp.zeros((segments * CAP,), jnp.int32).at[slot_index]]
  transfers between devices with their start and end apart: 7 -> 4, of which waited for: 3 -> 4; matrix products, arithmetic and copies ran while one was open for 30% -> 0% of each run, Pallas kernels for 0% -> 0%
where the time goes in v1:
time: 78.2 us; the launch traced here: 78 us
  Pallas kernels  37.3 us (48%)
  waiting for transfers between devices  18.1 us (23%)
  other arithmetic  9.44 us (12%)
  starting transfers between devices  9.11 us (12%)
  matrix products  3.1 us (4%)
  local copies, waits for them, and re-layouts  0.83 us (1%)
    pallas_call x1, Pallas kernels, sum_lags(): pl.pallas_call(functools.partial(sum_kernel, segments, bands), out_shape=...  21.1 us
    pallas_call x1, Pallas kernels, stack_pairs(): pl.pallas_call(functools.partial(pair_kernel, local_bins, bins), out_shap...  16.2 us
    ppermute x2, waiting for transfers between devices, extended(): lax.ppermute(lax.slice_in_dim(block, block.shape[dim] - width, None, axis...  9.97 us
    ppermute x2, waiting for transfers between devices, extended(): lax.ppermute(lax.slice_in_dim(block, 0, width, axis=dim), axis, backward)  8.16 us
    concatenate x1, other arithmetic, extended(): block = jnp.concatenate([low, block, high], axis=dim)  6.4 us
    ppermute x2, starting transfers between devices, extended(): lax.ppermute(lax.slice_in_dim(block, block.shape[dim] - width, None, axis...  6.34 us
    dot_general x1, matrix products, per_device(): jnp.dot(padded_power, window_matrix(local_bins, HALF_WIN), precision=lax....  3.1 us
    ppermute x2, starting transfers between devices, extended(): lax.ppermute(lax.slice_in_dim(block, 0, width, axis=dim), axis, backward)  2.76 us
  transfers between devices with their start and end apart: 4, of which 4 were waited for; matrix products, arithmetic and copies ran while one was open for 0% of the time, Pallas kernels for 0%

profile of v1, /device:TPU:0, one launch (start us, length us, event | category | flops | bytes accessed | tf_op | source)
XLA Modules:
  0.0 78.0 jit_solution(6433013211346605202)
XLA Ops:
  0.0 1.9 %fusion.6 = f32[1024,512]{1,0:T(8,128)S(1)} fusion(bf16[2,1024,512]{2,1,0:T(8,128)(2,1)} %param.4), kind=kLoop, calls=%fused_computation.11 | loop fusion | flops 2621440 | bytes 4194304 | tf_op jit(solution)/shard_map/add | solution.py:239
  1.9 0.0 copy-start
  1.9 0.2 fusion.13
  2.1 5.0 %collective-permute-start = (f32[1024,64]{1,0:T(8,128)S(1)}, f32[1024,64]{1,0:T(8,128)S(1)}, u32[]{:S(2)}, u32[]{:S(2)}) collective-permute-start(f32[1024,64]{1,0:T(8,128)S(1)} %get-tuple-element.9), channel_id=1, source_target_pairs={{0,1},{2,3},{4,5},{6,7},{8,9},{10,11},{12,13},{14,15},{16,17},{18,... | collective-permute-start | bytes 786440 | tf_op jit(solution)/shard_map/ppermute | solution.py:30
  7.2 1.3 %collective-permute-start.1 = (f32[1024,64]{1,0:T(8,128)S(1)}, f32[1024,64]{1,0:T(8,128)S(1)}, u32[]{:S(2)}, u32[]{:S(2)}) collective-permute-start(f32[1024,64]{1,0:T(8,128)S(1)} %get-tuple-element.10), channel_id=1, source_target_pairs={{1,0},{3,2},{5,4},{7,6},{9,8},{11,10},{13,12},{15,14},{17,16},{19,... | collective-permute-start | bytes 786440 | tf_op jit(solution)/shard_map/ppermute | solution.py:33
  8.5 9.8 %collective-permute-done = f32[1024,64]{1,0:T(8,128)S(1)} collective-permute-done((f32[1024,64]{1,0:T(8,128)S(1)}, f32[1024,64]{1,0:T(8,128)S(1)}, u32[]{:S(2)}, u32[]{:S(2)}) %collective-permute-start) | collective-permute-done | bytes 262176 | tf_op jit(solution)/shard_map/ppermute | solution.py:30
  18.3 4.1 %collective-permute-done.1 = f32[1024,64]{1,0:T(8,128)S(1)} collective-permute-done((f32[1024,64]{1,0:T(8,128)S(1)}, f32[1024,64]{1,0:T(8,128)S(1)}, u32[]{:S(2)}, u32[]{:S(2)}) %collective-permute-start.1) | collective-permute-done | bytes 262176 | tf_op jit(solution)/shard_map/ppermute | solution.py:33
  22.4 0.0 copy-done
  22.4 3.1 %fusion.7 = (bf16[1024,512]{1,0:T(8,128)(2,1)S(1)}, bf16[1024,512]{1,0:T(8,128)(2,1)S(1)}) fusion(bf16[2,1024,512]{2,1,0:T(8,128)(2,1)S(1)} %copy-done, s32[512]{0:T(512)S(1)} %iota_add_fusion, f32[1024,64]{1,0:T(8,128)S(1)} %collective-permute-done.1, f32[1024,512]{1,0:T(8,128)S(1)} %fusion.6, f32[1024,64]{1,0:T(8,128)S(1)} %collective-permute-done), kind=kOutput, calls=%fused_computation.12 | convolution fusion | flops 4033019904 | bytes 6817792 | tf_op jit(solution)/shard_map/dot_general | solution.py:241
  25.6 0.0 copy-start.1
  25.6 0.0 copy-start.2
  25.6 0.0 copy-start.3
  25.6 1.1 %pad_maximum_fusion.2 = (bf16[256,1024]{1,0:T(8,128)(2,1)}, bf16[256,1024]{1,0:T(8,128)(2,1)}) fusion(bf16[1024,512]{1,0:T(8,128)(2,1)S(1)} %get-tuple-element.6, bf16[1024,512]{1,0:T(8,128)(2,1)S(1)} %get-tuple-element.5), kind=kLoop, calls=%fused_computation.20 | loop fusion | flops 2097152 | bytes 3145728 | tf_op jit(solution)/shard_map/slice | solution.py:31
  26.7 1.3 %collective-permute-start.2 = (bf16[256,1024]{1,0:T(8,128)(2,1)}, bf16[256,1024]{1,0:T(8,128)(2,1)S(1)}, u32[]{:S(2)}, u32[]{:S(2)}) collective-permute-start(bf16[256,1024]{1,0:T(8,128)(2,1)} %get-tuple-element.7), channel_id=1, source_target_pairs={{0,2},{2,4},{4,6},{6,8},{8,10},{10,12},{12,14},{14,16},{16,18},{18... | collective-permute-start | bytes 1572872 | tf_op jit(solution)/shard_map/ppermute | solution.py:30
  28.0 1.5 %collective-permute-start.3 = (bf16[256,1024]{1,0:T(8,128)(2,1)}, bf16[256,1024]{1,0:T(8,128)(2,1)S(1)}, u32[]{:S(2)}, u32[]{:S(2)}) collective-permute-start(bf16[256,1024]{1,0:T(8,128)(2,1)} %get-tuple-element.8), channel_id=1, source_target_pairs={{2,0},{4,2},{6,4},{8,6},{10,8},{12,10},{14,12},{16,14},{18,16},{20... | collective-permute-start | bytes 1572872 | tf_op jit(solution)/shard_map/ppermute | solution.py:33
  29.5 0.0 copy-done.1
  29.5 0.0 copy-done.2
  29.6 0.0 copy-done.3
  29.6 0.2 collective-permute-done.2
  29.7 4.0 %collective-permute-done.3 = bf16[256,1024]{1,0:T(8,128)(2,1)S(1)} collective-permute-done((bf16[256,1024]{1,0:T(8,128)(2,1)}, bf16[256,1024]{1,0:T(8,128)(2,1)S(1)}, u32[]{:S(2)}, u32[]{:S(2)}) %collective-permute-start.3) | collective-permute-done | bytes 524320 | tf_op jit(solution)/shard_map/ppermute | solution.py:33
  33.8 6.4 %pad_maximum_fusion.white_ref = bf16[1536,1024]{1,0:T(8,128)(2,1)S(1)} fusion(bf16[256,1024]{1,0:T(8,128)(2,1)S(1)} %collective-permute-done.3, bf16[1024,512]{1,0:T(8,128)(2,1)S(1)} %get-tuple-element.6, bf16[1024,512]{1,0:T(8,128)(2,1)S(1)} %get-tuple-element.5, bf16[256,1024]{1,0:T(8,128)(2,1)S(1)} %collective-permute-done.2), kind=kLoop, calls=%fused_computation | loop fusion | flops 12582912 | bytes 6291456 | tf_op jit(solution)/shard_map/concatenate | solution.py:34
  40.2 16.2 %pairs.1.lags_ref = f32[128,1024]{1,0:T(8,128)S(1)} custom-call(s32[4096]{0:T(1024)S(1)} %get-tuple-element.12.first_ref, s32[4096]{0:T(1024)S(1)} %get-tuple-element.11.second_ref, s32[4096]{0:T(1024)S(1)} %broadcast_multiply_fusion.bin_ref, bf16[1536,1024]{1,0:T(8,128)(2,1)S(1)} %pad_maximum_fusion.white_ref), custom_call_target="tpu_custom_call" | custom-call | tf_op jit(solution)/shard_map/pairs/pallas_call | solution.py:191
  56.3 21.1 %sums.1 = f32[8,512]{1,0:T(8,128)S(1)} custom-call(f32[128,1024]{1,0:T(8,128)S(1)} %pairs.1.lags_ref), custom_call_target="tpu_custom_call" | custom-call | tf_op jit(solution)/shard_map/sums/pallas_call | solution.py:211
  77.4 0.6 copy.8
  (3 shorter events, 0.0 us)
Async XLA Ops:
  1.9 20.5 %copy-start = (bf16[2,1024,512]{2,1,0:T(8,128)(2,1)S(1)}, bf16[2,1024,512]{2,1,0:T(8,128)(2,1)}, u32[]{:S(2)}) copy-start(bf16[2,1024,512]{2,1,0:T(8,128)(2,1)} %param.4) | copy-start | bytes 6291460
  2.1 16.2 %collective-permute-start = (f32[1024,64]{1,0:T(8,128)S(1)}, f32[1024,64]{1,0:T(8,128)S(1)}, u32[]{:S(2)}, u32[]{:S(2)}) collective-permute-start(f32[1024,64]{1,0:T(8,128)S(1)} %get-tuple-element.9), channel_id=1, source_target_pairs={{0,1},{2,3},{4,5},{6,7},{8,9},{10,11},{12,13},{14,15},{16,17},{18,... | collective-permute-start | bytes 786440 | tf_op jit(solution)/shard_map/ppermute | solution.py:30
  7.2 15.3 %collective-permute-start.1 = (f32[1024,64]{1,0:T(8,128)S(1)}, f32[1024,64]{1,0:T(8,128)S(1)}, u32[]{:S(2)}, u32[]{:S(2)}) collective-permute-start(f32[1024,64]{1,0:T(8,128)S(1)} %get-tuple-element.10), channel_id=1, source_target_pairs={{1,0},{3,2},{5,4},{7,6},{9,8},{11,10},{13,12},{15,14},{17,16},{19,... | collective-permute-start | bytes 786440 | tf_op jit(solution)/shard_map/ppermute | solution.py:33
  25.6 4.0 %copy-start.1 = (s32[4096]{0:T(1024)S(1)}, s32[4096]{0:T(1024)}, u32[]{:S(2)}) copy-start(s32[4096]{0:T(1024)} %param.7) | copy-start | bytes 49156
  25.6 4.0 %copy-start.2 = (s32[4096]{0:T(1024)S(1)}, s32[4096]{0:T(1024)}, u32[]{:S(2)}) copy-start(s32[4096]{0:T(1024)} %param.6) | copy-start | bytes 49156
  25.6 4.0 %copy-start.3 = (s32[4096]{0:T(1024)S(1)}, s32[4096]{0:T(1024)}, u32[]{:S(2)}) copy-start(s32[4096]{0:T(1024)} %param.5) | copy-start | bytes 49156
  26.7 3.0 %collective-permute-start.2 = (bf16[256,1024]{1,0:T(8,128)(2,1)}, bf16[256,1024]{1,0:T(8,128)(2,1)S(1)}, u32[]{:S(2)}, u32[]{:S(2)}) collective-permute-start(bf16[256,1024]{1,0:T(8,128)(2,1)} %get-tuple-element.7), channel_id=1, source_target_pairs={{0,2},{2,4},{4,6},{6,8},{8,10},{10,12},{12,14},{14,16},{16,18},{18... | collective-permute-start | bytes 1572872 | tf_op jit(solution)/shard_map/ppermute | solution.py:30
  28.0 5.7 %collective-permute-start.3 = (bf16[256,1024]{1,0:T(8,128)(2,1)}, bf16[256,1024]{1,0:T(8,128)(2,1)S(1)}, u32[]{:S(2)}, u32[]{:S(2)}) collective-permute-start(bf16[256,1024]{1,0:T(8,128)(2,1)} %get-tuple-element.8), channel_id=1, source_target_pairs={{2,0},{4,2},{6,4},{8,6},{10,8},{12,10},{14,12},{16,14},{18,16},{20... | collective-permute-start | bytes 1572872 | tf_op jit(solution)/shard_map/ppermute | solution.py:33

commit v2 on v1

--- a/solution.py
+++ b/solution.py
@@ -22,26 +22,6 @@
 epsilon = 1e-06
 
 
-def extended(block, sides, width):
-    for axis, dim in sides:
-        count = lax.axis_size(axis)
-        forward = [(i, i + 1) for i in range(count - 1)]
-        backward = [(target, source) for source, target in forward]
-        low = lax.ppermute(
-            lax.slice_in_dim(block, block.shape[dim] - width, None, axis=dim), axis, forward
-        )
-        high = lax.ppermute(lax.slice_in_dim(block, 0, width, axis=dim), axis, backward)
-        block = jnp.concatenate([low, block, high], axis=dim)
-    return block
-
-
-def window_matrix(local_bins, half_width):
-    padded_index = jnp.arange(local_bins + 2 * half_width)[:, None]
-    bin_index = jnp.arange(local_bins)[None, :]
-    inside = (padded_index >= bin_index) & (padded_index <= bin_index + 2 * half_width)
-    return inside.astype(jnp.float32)
-
-
 def circle(first, step, count):
     rows = lax.broadcasted_iota(jnp.int32, (count, LAGS), 0) * step + first
     lags = lax.broadcasted_iota(jnp.int32, (count, LAGS), 1) - LAGS // 2
@@ -63,19 +43,184 @@
         ).astype(jnp.bfloat16)
 
 
+def whiten_kernel(
+    segments, bands, spectra_ref, first_ref, second_ref, bin_ref,
+    rows, table, first_out, second_out, bin_out,
+    near, window, edge_out, left_in, right_in, load_sem, send_sem, recv_sem,
+):
+    channels, local_bins = spectra_ref.shape[1:]
+    groups = channels // REACH
+    parts = 2 * local_bins // LANES
+    half = parts // 2
+    packed = REACH // 2
+    seg, band = lax.axis_index("seg"), lax.axis_index("band")
+
+    seg_there = {-1: seg > 0, 0: None, 1: seg < segments - 1}
+    band_there = {-1: band > 0, 0: None, 1: band < bands - 1}
+    peers = [(ds, db) for ds in (-1, 0, 1) for db in (-1, 0, 1) if (ds, db) != (0, 0)]
+
+    def there(ds, db):
+        if ds == 0:
+            return band_there[db]
+        if db == 0:
+            return seg_there[ds]
+        return jnp.logical_and(seg_there[ds], band_there[db])
+
+    load = pltpu.make_async_copy(
+        spectra_ref, near.at[:, pl.ds(REACH, channels), :], load_sem.at[0]
+    )
+    load.start()
+    barrier = pltpu.get_barrier_semaphore()
+    for ds, db in peers:
+        @pl.when(there(ds, db))
+        def _():
+            pl.semaphore_signal(
+                barrier, inc=1, device_id=(seg + ds, band + db), device_id_type=MESH
+            )
+    seg_span = 3 - jnp.where(seg == 0, 1, 0) - jnp.where(seg == segments - 1, 1, 0)
+    band_span = 3 - jnp.where(band == 0, 1, 0) - jnp.where(band == bands - 1, 1, 0)
+    pl.semaphore_wait(barrier, seg_span * band_span - 1)
+
+    def sending(ds, db):
+        slot = peers.index((ds, db))
+        if db == 0:
+            source = spectra_ref.at[:, pl.ds(channels - REACH if ds > 0 else 0, REACH), :]
+            target = near.at[:, pl.ds(0 if ds > 0 else REACH + channels, REACH), :]
+        else:
+            side, box = (1, left_in) if db > 0 else (0, right_in)
+            if ds == 0:
+                source = edge_out.at[side]
+                target = box.at[pl.ds(1, groups)]
+            else:
+                source = edge_out.at[side, pl.ds(groups - 1 if ds > 0 else 0, 1)]
+                target = box.at[pl.ds(0 if ds > 0 else groups + 1, 1)]
+        return pltpu.make_async_remote_copy(
+            src_ref=source, dst_ref=target, send_sem=send_sem.at[slot],
+            recv_sem=recv_sem.at[slot], device_id=(seg + ds, band + db), device_id_type=MESH,
+        )
+
+    def start(ds, db):
+        @pl.when(there(ds, db))
+        def _():
+            sending(ds, db).start()
+
+    def arrived(ds, db):
+        @pl.when(there(-ds, -db))
+        def _():
+            sending(ds, db).wait_recv()
+
+    start(-1, 0)
+    start(1, 0)
+    load.wait()
+
+    lane = lax.broadcasted_iota(jnp.int32, (packed, LANES), 1)
+
+    def edge(side, group):
+        at = 0 if side == 0 else local_bins - LANES
+        real = near[0, pl.ds(REACH + group * REACH, REACH), at : at + LANES].astype(jnp.float32)
+        imag = near[1, pl.ds(REACH + group * REACH, REACH), at : at + LANES].astype(jnp.float32)
+        power = real * real + imag * imag
+        upper, lower = power[:packed], power[packed:]
+        if side == 0:
+            both = jnp.where(lane < HALF_WIN, upper, pltpu.roll(lower, HALF_WIN, 1))
+        else:
+            both = jnp.where(lane < HALF_WIN, pltpu.roll(upper, HALF_WIN, 1), lower)
+        edge_out[side, group] = both.astype(jnp.bfloat16)
+
+    for side, db in ((0, -1), (1, 1)):
+        @pl.when(band_there[db])
+        def _():
+            for group in range(groups):
+                edge(side, group)
+        start(0, db)
+        start(-1, db)
+        start(1, db)
+    for db, box in ((-1, left_in), (1, right_in)):
+        @pl.when(jnp.logical_not(band_there[db]))
+        def _():
+            box[...] = jnp.zeros_like(box)
+
+    shift = REACH - seg * channels
+    first_out[...] = (first_ref[...] + shift) * parts
+    second_out[...] = (second_ref[...] + shift) * parts
+    bin_out[...] = bin_ref[...] * (2 * parts)
+    distance = lax.broadcasted_iota(jnp.int32, (local_bins, local_bins), 0) - (
+        lax.broadcasted_iota(jnp.int32, (local_bins, local_bins), 1)
+    )
+    window[...] = (jnp.abs(distance) <= HALF_WIN).astype(jnp.float32).astype(jnp.bfloat16)
+    write_basis(band * local_bins, local_bins, table)
+
+    source = lax.broadcasted_iota(jnp.int32, (LANES, LANES), 0)
+    column = lax.broadcasted_iota(jnp.int32, (LANES, LANES), 1)
+
+    def chosen(inside):
+        return inside.astype(jnp.float32).astype(jnp.bfloat16)
+
+    left_weights = [
+        chosen((source < HALF_WIN) & (column <= source)),
+        chosen((source >= HALF_WIN) & (column <= source - HALF_WIN)),
+    ]
+    right_weights = [
+        chosen((source < HALF_WIN) & (column >= source + HALF_WIN)),
+        chosen((source >= HALF_WIN) & (column >= source)),
+    ]
+
+    def dot(a, b):
+        return jnp.dot(a, b, preferred_element_type=jnp.float32)
+
+    def outside(box, group, weights):
+        values = box[group]
+        return jnp.concatenate([dot(values, weights[0]), dot(values, weights[1])], axis=0)
+
+    def whiten(group):
+        at = pl.ds(pl.multiple_of(group * REACH, REACH), REACH)
+        real = near[0, at, :].astype(jnp.float32)
+        imag = near[1, at, :].astype(jnp.float32)
+        power = real * real + imag * imag
+        high = power.astype(jnp.bfloat16)
+        low = (power - high.astype(jnp.float32)).astype(jnp.bfloat16)
+        total = dot(high, window[...]) + dot(low, window[...])
+        for j in range(half):
+            columns = slice(j * LANES, (j + 1) * LANES)
+            piece = total[:, columns]
+            if j == 0:
+                piece = piece + outside(left_in, group, left_weights)
+            if j == half - 1:
+                piece = piece + outside(right_in, group, right_weights)
+            scaling = lax.rsqrt(piece / (2 * HALF_WIN + 1) + epsilon)
+            for k, part in ((0, real), (1, imag)):
+                white = (part[:, columns] * scaling).astype(jnp.bfloat16).astype(jnp.float32)
+                rows[pl.ds(group * (REACH * parts) + k * half + j, REACH, stride=parts), :] = white
+
+    for db in (-1, 1):
+        arrived(0, db)
+
+    def local(group, carry):
+        whiten(group)
+        return carry
+
+    lax.fori_loop(1, groups + 1, local, 0)
+    for ds, group in ((1, 0), (-1, groups + 1)):
+        arrived(ds, 0)
+        arrived(ds, -1)
+        arrived(ds, 1)
+
+        @pl.when(seg_there[-ds])
+        def _():
+            whiten(group)
+    for ds, db in peers:
+        @pl.when(there(ds, db))
+        def _():
+            sending(ds, db).wait_send()
+
+
 def pair_kernel(
-    local_bins, bins, first_ref, second_ref, bin_ref, white_ref, out_ref, rows, table, *banks
+    local_bins, bins, first_ref, second_ref, bin_ref, rows, table, out_ref, *banks
 ):
     parts = 2 * local_bins // LANES
     half = parts // 2
-    channels = white_ref.shape[0]
-    write_basis(lax.axis_index("band") * local_bins, local_bins, table)
     for bank in banks:
         bank[...] = jnp.zeros_like(bank)
-    for j in range(parts):
-        rows[pl.ds(j, channels, stride=parts), :] = white_ref[
-            :, j * LANES : (j + 1) * LANES
-        ].astype(jnp.float32)
 
     def group(step, carry):
         base = step * BANKS
@@ -184,23 +329,54 @@
         far_copy(d).wait_send()
 
 
-def stack_pairs(white, first, second, bins_at, local_bins, bins):
+def whiten(spectra, first, second, bins_at, segments, bands):
+    _, channels, local_bins = spectra.shape
+    parts = 2 * local_bins // LANES
+    groups = channels // REACH
+    count = first.shape[0]
+    boxed = (count // LANES, LANES)
+    vmem = pl.BlockSpec(memory_space=pltpu.VMEM)
+    dma = pltpu.SemaphoreType.DMA
+    edges = (groups + 2, REACH // 2, LANES)
+    index = jax.ShapeDtypeStruct(boxed, jnp.int32)
+    rows, table, *indices = pl.pallas_call(
+        functools.partial(whiten_kernel, segments, bands),
+        out_shape=[
+            jax.ShapeDtypeStruct(((channels + 2 * REACH) * parts, LANES), jnp.float32),
+            jax.ShapeDtypeStruct((2 * local_bins, LAGS), jnp.bfloat16),
+            index, index, index,
+        ],
+        in_specs=[pl.BlockSpec(memory_space=pl.ANY), vmem, vmem, vmem],
+        out_specs=[vmem] * 5,
+        scratch_shapes=[
+            pltpu.VMEM((2, channels + 2 * REACH, local_bins), jnp.bfloat16),
+            pltpu.VMEM((local_bins, local_bins), jnp.bfloat16),
+            pltpu.VMEM((2, groups) + edges[1:], jnp.bfloat16),
+            pltpu.VMEM(edges, jnp.bfloat16),
+            pltpu.VMEM(edges, jnp.bfloat16),
+            dma((1,)), dma((8,)), dma((8,)),
+        ],
+        compiler_params=pltpu.CompilerParams(
+            collective_id=0, has_side_effects=True, vmem_limit_bytes=32 * 2**20
+        ),
+        name="whiten",
+    )(spectra, first.reshape(boxed), second.reshape(boxed), bins_at.reshape(boxed))
+    return rows, table, [x.reshape(count) for x in indices]
+
+
+def stack_pairs(rows, table, indices, local_bins, bins):
     parts = 2 * local_bins // LANES
     smem = pl.BlockSpec(memory_space=pltpu.SMEM)
     vmem = pl.BlockSpec(memory_space=pltpu.VMEM)
     return pl.pallas_call(
         functools.partial(pair_kernel, local_bins, bins),
         out_shape=jax.ShapeDtypeStruct((bins, LAGS), jnp.float32),
-        in_specs=[smem, smem, smem, vmem],
+        in_specs=[smem, smem, smem, vmem, vmem],
         out_specs=vmem,
-        scratch_shapes=[
-            pltpu.VMEM((white.shape[0] * parts, LANES), jnp.float32),
-            pltpu.VMEM((2 * local_bins, LAGS), jnp.bfloat16),
-        ]
-        + [pltpu.VMEM((bins * 2 * parts, LANES), jnp.float32)] * BANKS,
-        compiler_params=pltpu.CompilerParams(vmem_limit_bytes=48 * 2**20),
+        scratch_shapes=[pltpu.VMEM((bins * 2 * parts, LANES), jnp.float32)] * BANKS,
+        compiler_params=pltpu.CompilerParams(vmem_limit_bytes=32 * 2**20),
         name="pairs",
-    )(first, second, bins_at, white)
+    )(*indices, rows, table)
 
 
 def sum_lags(lags, segments, bands):
@@ -228,33 +404,9 @@
 
 
 def per_device(spectra, pair_first, pair_second, pair_bin):
-    seg_position = lax.axis_index("seg")
-    segments = lax.axis_size("seg")
-    bands = lax.axis_size("band")
-    channels = spectra.shape[1]
-    local_bins = spectra.shape[2]
-    parts = 2 * local_bins // LANES
-    real_part = spectra[0].astype(jnp.float32)
-    imag_part = spectra[1].astype(jnp.float32)
-    power_sum = real_part * real_part + imag_part * imag_part
-    padded_power = extended(power_sum, (("band", 1),), HALF_WIN)
-    window_sum = jnp.dot(
-        padded_power, window_matrix(local_bins, HALF_WIN), precision=lax.Precision.HIGHEST
-    )
-    scaling = lax.rsqrt(window_sum / (2 * HALF_WIN + 1) + epsilon)
-    whitened = jnp.concatenate([real_part * scaling, imag_part * scaling], axis=1).astype(
-        jnp.bfloat16
-    )
-    near_rows = extended(whitened, (("seg", 0),), REACH)
-    shift = REACH - seg_position * channels
-    lags = stack_pairs(
-        near_rows,
-        (pair_first + shift) * parts,
-        (pair_second + shift) * parts,
-        pair_bin * (2 * parts),
-        local_bins,
-        segments * OB_DEV,
-    )
+    segments, bands = lax.axis_size("seg"), lax.axis_size("band")
+    rows, table, indices = whiten(spectra, pair_first, pair_second, pair_bin, segments, bands)
+    lags = stack_pairs(rows, table, indices, spectra.shape[2], segments * OB_DEV)
     return sum_lags(lags, segments, bands)
 
 

time: 78.2 us -> 48.2 us (0.62)
  waiting for transfers between devices: 18.1 us -> 0 us
  other arithmetic: 9.44 us -> 0 us
  starting transfers between devices: 9.11 us -> 0 us
  Pallas kernels: 37.3 us -> 43.4 us
  local copies, waits for them, and re-layouts: 0.83 us -> 4.35 us
  matrix products: 3.1 us -> 0 us
    ppermute x4 -> x0, waiting for transfers between devices: 18.1 us -> none  [the longest x2 9.97 us: extended(): lax.ppermute(lax.slice_in_dim(block, block.shape[dim] - width, None, axis...]
    pallas_call x0 -> x1, Pallas kernels: none -> 10.2 us  [whiten(): pl.pallas_call(functools.partial(whiten_kernel, segments, bands), out_sha...]
    ppermute x4 -> x0, starting transfers between devices: 9.11 us -> none  [the longest x2 6.34 us: extended(): lax.ppermute(lax.slice_in_dim(block, block.shape[dim] - width, None, axis...]
    concatenate x1 -> x0, other arithmetic: 6.4 us -> none  [extended(): block = jnp.concatenate([low, block, high], axis=dim)]
    unnamed x9, local copies, waits for them, and re-layouts: 0.63 us -> 4.35 us
    pallas_call x1, Pallas kernels: 16.2 us -> 12.9 us  [stack_pairs(): pl.pallas_call(functools.partial(pair_kernel, local_bins, bins), out_shap...]
    dot_general x1 -> x0, matrix products: 3.1 us -> none  [per_device(): jnp.dot(padded_power, window_matrix(local_bins, HALF_WIN), precision=lax....]
    add x2 -> x0, other arithmetic: 1.91 us -> none  [the longest x1 1.9 us: per_device(): power_sum = real_part * real_part + imag_part * imag_part]
  transfers between devices with their start and end apart: 4 -> 0, of which waited for: 4 -> 0; matrix products, arithmetic and copies ran while one was open for 0% -> 0% of each run, Pallas kernels for 0% -> 0%
where the time goes in v2:
time: 48.2 us; the launch traced here: 47.8 us
  Pallas kernels  43.4 us (90%)
  local copies, waits for them, and re-layouts  4.35 us (9%)
    pallas_call x1, Pallas kernels, sum_lags(): pl.pallas_call(functools.partial(sum_kernel, segments, bands), out_shape=...  20.3 us
    pallas_call x1, Pallas kernels, stack_pairs(): pl.pallas_call(functools.partial(pair_kernel, local_bins, bins), out_shap...  12.9 us
    pallas_call x1, Pallas kernels, whiten(): pl.pallas_call(functools.partial(whiten_kernel, segments, bands), out_sha...  10.2 us
    unnamed x9, local copies, waits for them, and re-layouts  4.35 us

profile of v2, /device:TPU:0, one launch (start us, length us, event | category | flops | bytes accessed | tf_op | source)
XLA Modules:
  0.0 47.8 jit_solution(6871425400983738060)
XLA Ops:
  0.0 0.0 copy-start
  0.0 1.6 %copy-done = bf16[2,1024,512]{2,1,0:T(8,128)(2,1)S(1)} copy-done((bf16[2,1024,512]{2,1,0:T(8,128)(2,1)S(1)}, bf16[2,1024,512]{2,1,0:T(8,128)(2,1)}, u32[]{:S(2)}) %copy-start) | copy-done | bytes 2097176
  1.6 0.0 copy-start.1
  1.6 0.7 %copy-done.1 = s32[4096]{0:T(1024)S(1)} copy-done((s32[4096]{0:T(1024)S(1)}, s32[4096]{0:T(1024)}, u32[]{:S(2)}) %copy-start.1) | copy-done | bytes 16408
  2.3 0.0 copy-start.2
  2.3 0.7 %copy-done.2 = s32[4096]{0:T(1024)S(1)} copy-done((s32[4096]{0:T(1024)S(1)}, s32[4096]{0:T(1024)}, u32[]{:S(2)}) %copy-start.2) | copy-done | bytes 16408
  3.0 0.0 copy-start.3
  3.0 0.7 %copy-done.3 = s32[4096]{0:T(1024)S(1)} copy-done((s32[4096]{0:T(1024)S(1)}, s32[4096]{0:T(1024)}, u32[]{:S(2)}) %copy-start.3) | copy-done | bytes 16408
  3.7 10.2 %whiten.1 = (f32[12288,128]{1,0:T(8,128)S(1)}, bf16[1024,1024]{1,0:T(8,128)(2,1)S(1)}, s32[32,128]{1,0:T(8,128)S(1)}, s32[32,128]{1,0:T(8,128)S(1)}, s32[32,128]{1,0:T(8,128)S(1)}) custom-call(bf16[2,1024,512]{2,1,0:T(8,128)(2,1)S(1)} %copy-done, s32[32,128]{1,0:T(8,128)S(1)} %bitcast.6, s32[32,128]{1,0:T(8,128)S(1)} %bitcast.7, s32[32,128]{1,0:T(8,128)S(1)} %bitcast.8), custom_call_target="tpu_custom_call" | custom-call | tf_op jit(solution)/shard_map/whiten/pallas_call | solution.py:342
  13.9 12.9 %pairs.1.lags_ref = f32[128,1024]{1,0:T(8,128)S(1)} custom-call(s32[4096]{0:T(1024)S(1)} %bitcast.9, s32[4096]{0:T(1024)S(1)} %bitcast.10, s32[4096]{0:T(1024)S(1)} %bitcast.11, f32[12288,128]{1,0:T(8,128)S(1)} %get-tuple-element.13.rows, bf16[1024,1024]{1,0:T(8,128)(2,1)S(1)} %get-tuple-element.14.table), custom_call_target="tpu_custom_call" | custom-call | tf_op jit(solution)/shard_map/pairs/pallas_call | solution.py:371
  26.8 20.3 %sums.1 = f32[8,512]{1,0:T(8,128)S(1)} custom-call(f32[128,1024]{1,0:T(8,128)S(1)} %pairs.1.lags_ref), custom_call_target="tpu_custom_call" | custom-call | tf_op jit(solution)/shard_map/sums/pallas_call | solution.py:387
  47.2 0.6 %copy.6 = f32[8,512]{1,0:T(8,128)} copy(f32[8,512]{1,0:T(8,128)S(1)} %sums.1) | data formatting | bytes 32768
Async XLA Ops:
  0.0 1.6 %copy-start = (bf16[2,1024,512]{2,1,0:T(8,128)(2,1)S(1)}, bf16[2,1024,512]{2,1,0:T(8,128)(2,1)}, u32[]{:S(2)}) copy-start(bf16[2,1024,512]{2,1,0:T(8,128)(2,1)} %spectra_ref.1) | copy-start | bytes 6291460
  1.6 0.7 %copy-start.1 = (s32[4096]{0:T(1024)S(1)}, s32[4096]{0:T(1024)}, u32[]{:S(2)}) copy-start(s32[4096]{0:T(1024)} %param.5) | copy-start | bytes 49156
  2.3 0.7 %copy-start.2 = (s32[4096]{0:T(1024)S(1)}, s32[4096]{0:T(1024)}, u32[]{:S(2)}) copy-start(s32[4096]{0:T(1024)} %param.6) | copy-start | bytes 49156
  3.0 0.7 %copy-start.3 = (s32[4096]{0:T(1024)S(1)}, s32[4096]{0:T(1024)}, u32[]{:S(2)}) copy-start(s32[4096]{0:T(1024)} %param.7) | copy-start | bytes 49156

commit v3 on v2

--- a/solution.py
+++ b/solution.py
@@ -13,7 +13,7 @@
 FREQ = 1024
 LAGS = 1024
 HALF_WIN = 64
-BANKS = 4
+BANKS = 8
 LANES = 128
 FINE = 32
 NEAR_SEGS = 4
@@ -46,7 +46,7 @@
 def whiten_kernel(
     segments, bands, spectra_ref, first_ref, second_ref, bin_ref,
     rows, table, first_out, second_out, bin_out,
-    near, window, edge_out, left_in, right_in, load_sem, send_sem, recv_sem,
+    near, window, edge_out, left_in, right_in, index_in, load_sem, send_sem, recv_sem,
 ):
     channels, local_bins = spectra_ref.shape[1:]
     groups = channels // REACH
@@ -70,6 +70,12 @@
         spectra_ref, near.at[:, pl.ds(REACH, channels), :], load_sem.at[0]
     )
     load.start()
+    index_loads = [
+        pltpu.make_async_copy(ref, index_in.at[k], load_sem.at[1 + k])
+        for k, ref in enumerate((first_ref, second_ref, bin_ref))
+    ]
+    for index_load in index_loads:
+        index_load.start()
     barrier = pltpu.get_barrier_semaphore()
     for ds, db in peers:
         @pl.when(there(ds, db))
@@ -141,9 +147,11 @@
             box[...] = jnp.zeros_like(box)
 
     shift = REACH - seg * channels
-    first_out[...] = (first_ref[...] + shift) * parts
-    second_out[...] = (second_ref[...] + shift) * parts
-    bin_out[...] = bin_ref[...] * (2 * parts)
+    for index_load in index_loads:
+        index_load.wait()
+    first_out[...] = (index_in[0] + shift) * parts
+    second_out[...] = (index_in[1] + shift) * parts
+    bin_out[...] = index_in[2] * parts
     distance = lax.broadcasted_iota(jnp.int32, (local_bins, local_bins), 0) - (
         lax.broadcasted_iota(jnp.int32, (local_bins, local_bins), 1)
     )
@@ -222,37 +230,33 @@
     for bank in banks:
         bank[...] = jnp.zeros_like(bank)
 
+    upper = lax.broadcasted_iota(jnp.int32, (parts, LANES), 0) < half
+
     def group(step, carry):
         base = step * BANKS
         updates = []
         for k, bank in enumerate(banks):
             a = pl.multiple_of(first_ref[base + k], parts)
             b = pl.multiple_of(second_ref[base + k], parts)
-            o = pl.multiple_of(bin_ref[base + k], 2 * parts)
+            o = pl.multiple_of(bin_ref[base + k], parts)
             first = rows[pl.ds(a, parts), :]
             second = rows[pl.ds(b, parts), :]
-            straight = bank[pl.ds(o, parts), :] + first * second
-            crossed = bank[pl.ds(o + parts, parts), :] + pltpu.roll(first, half, 0) * second
-            updates.append((bank, o, straight, crossed))
-        for bank, o, straight, crossed in updates:
-            bank[pl.ds(o, parts), :] = straight
-            bank[pl.ds(o + parts, parts), :] = crossed
+            turned = pltpu.roll(second, half, 0)
+            real = jnp.where(upper, second, turned)
+            imag = jnp.where(upper, turned, -second)
+            cross = first * real + pltpu.roll(first, half, 0) * imag
+            updates.append((bank, o, bank[pl.ds(o, parts), :] + cross))
+        for bank, o, updated in updates:
+            bank[pl.ds(o, parts), :] = updated
         return carry
 
-    lax.fori_loop(0, first_ref.shape[0] // BANKS, group, 0, unroll=4)
-
-    def stacked(j):
-        total = banks[0][pl.ds(j, bins, stride=2 * parts), :]
-        for bank in banks[1:]:
-            total = total + bank[pl.ds(j, bins, stride=2 * parts), :]
-        return total
+    lax.fori_loop(0, first_ref.shape[0] // BANKS, group, 0, unroll=2)
 
     lags = jnp.zeros((bins, LAGS), jnp.float32)
     for j in range(parts):
-        if j < half:
-            piece = stacked(j) + stacked(half + j)
-        else:
-            piece = stacked(parts + j - half) - stacked(parts + j)
+        piece = banks[0][pl.ds(j, bins, stride=parts), :]
+        for bank in banks[1:]:
+            piece = piece + bank[pl.ds(j, bins, stride=parts), :]
         high = piece.astype(jnp.bfloat16)
         low = (piece - high.astype(jnp.float32)).astype(jnp.bfloat16)
         basis = table[j * LANES : (j + 1) * LANES, :]
@@ -346,7 +350,7 @@
             jax.ShapeDtypeStruct((2 * local_bins, LAGS), jnp.bfloat16),
             index, index, index,
         ],
-        in_specs=[pl.BlockSpec(memory_space=pl.ANY), vmem, vmem, vmem],
+        in_specs=[pl.BlockSpec(memory_space=pltpu.HBM)] * 4,
         out_specs=[vmem] * 5,
         scratch_shapes=[
             pltpu.VMEM((2, channels + 2 * REACH, local_bins), jnp.bfloat16),
@@ -354,7 +358,8 @@
             pltpu.VMEM((2, groups) + edges[1:], jnp.bfloat16),
             pltpu.VMEM(edges, jnp.bfloat16),
             pltpu.VMEM(edges, jnp.bfloat16),
-            dma((1,)), dma((8,)), dma((8,)),
+            pltpu.VMEM((3,) + boxed, jnp.int32),
+            dma((4,)), dma((8,)), dma((8,)),
         ],
         compiler_params=pltpu.CompilerParams(
             collective_id=0, has_side_effects=True, vmem_limit_bytes=32 * 2**20
@@ -373,7 +378,7 @@
         out_shape=jax.ShapeDtypeStruct((bins, LAGS), jnp.float32),
         in_specs=[smem, smem, smem, vmem, vmem],
         out_specs=vmem,
-        scratch_shapes=[pltpu.VMEM((bins * 2 * parts, LANES), jnp.float32)] * BANKS,
+        scratch_shapes=[pltpu.VMEM((bins * parts, LANES), jnp.float32)] * BANKS,
         compiler_params=pltpu.CompilerParams(vmem_limit_bytes=32 * 2**20),
         name="pairs",
     )(*indices, rows, table)

time: 48.2 us -> 48.4 us (level)
  no operation moved by 1% of the time
where the time goes in v3:
time: 48.4 us; the launch traced here: 48 us
  Pallas kernels  43.6 us (90%)
  local copies, waits for them, and re-layouts  4.35 us (9%)
    pallas_call x1, Pallas kernels, sum_lags(): pl.pallas_call(functools.partial(sum_kernel, segments, bands), out_shape=...  20.3 us
    pallas_call x1, Pallas kernels, stack_pairs(): pl.pallas_call(functools.partial(pair_kernel, local_bins, bins), out_shap...  13.1 us
    pallas_call x1, Pallas kernels, whiten(): pl.pallas_call(functools.partial(whiten_kernel, segments, bands), out_sha...  10.3 us
    unnamed x9, local copies, waits for them, and re-layouts  4.35 us

profile of v3, /device:TPU:0, one launch (start us, length us, event | category | flops | bytes accessed | tf_op | source)
XLA Modules:
  0.0 48.0 jit_solution(16666111865312275732)
XLA Ops:
  0.0 0.0 copy-start
  0.0 1.6 %copy-done = bf16[2,1024,512]{2,1,0:T(8,128)(2,1)S(1)} copy-done((bf16[2,1024,512]{2,1,0:T(8,128)(2,1)S(1)}, bf16[2,1024,512]{2,1,0:T(8,128)(2,1)}, u32[]{:S(2)}) %copy-start) | copy-done | bytes 2097176
  1.6 0.0 copy-start.1
  1.6 0.7 %copy-done.1 = s32[4096]{0:T(1024)S(1)} copy-done((s32[4096]{0:T(1024)S(1)}, s32[4096]{0:T(1024)}, u32[]{:S(2)}) %copy-start.1) | copy-done | bytes 16408
  2.3 0.0 copy-start.2
  2.3 0.7 %copy-done.2 = s32[4096]{0:T(1024)S(1)} copy-done((s32[4096]{0:T(1024)S(1)}, s32[4096]{0:T(1024)}, u32[]{:S(2)}) %copy-start.2) | copy-done | bytes 16408
  3.0 0.0 copy-start.3
  3.0 0.7 %copy-done.3 = s32[4096]{0:T(1024)S(1)} copy-done((s32[4096]{0:T(1024)S(1)}, s32[4096]{0:T(1024)}, u32[]{:S(2)}) %copy-start.3) | copy-done | bytes 16408
  3.7 10.3 %whiten.1 = (f32[12288,128]{1,0:T(8,128)S(1)}, bf16[1024,1024]{1,0:T(8,128)(2,1)S(1)}, s32[32,128]{1,0:T(8,128)S(1)}, s32[32,128]{1,0:T(8,128)S(1)}, s32[32,128]{1,0:T(8,128)S(1)}) custom-call(bf16[2,1024,512]{2,1,0:T(8,128)(2,1)S(1)} %copy-done, s32[32,128]{1,0:T(8,128)S(1)} %bitcast.6, s32[32,128]{1,0:T(8,128)S(1)} %bitcast.7, s32[32,128]{1,0:T(8,128)S(1)} %bitcast.8), custom_call_target="tpu_custom_call" | custom-call | tf_op jit(solution)/shard_map/whiten/pallas_call | solution.py:346
  14.0 13.1 %pairs.1.lags_ref = f32[128,1024]{1,0:T(8,128)S(1)} custom-call(s32[4096]{0:T(1024)S(1)} %bitcast.9, s32[4096]{0:T(1024)S(1)} %bitcast.10, s32[4096]{0:T(1024)S(1)} %bitcast.11, f32[12288,128]{1,0:T(8,128)S(1)} %get-tuple-element.13.rows, bf16[1024,1024]{1,0:T(8,128)(2,1)S(1)} %get-tuple-element.14.table), custom_call_target="tpu_custom_call" | custom-call | tf_op jit(solution)/shard_map/pairs/pallas_call | solution.py:376
  27.1 20.3 %sums.1 = f32[8,512]{1,0:T(8,128)S(1)} custom-call(f32[128,1024]{1,0:T(8,128)S(1)} %pairs.1.lags_ref), custom_call_target="tpu_custom_call" | custom-call | tf_op jit(solution)/shard_map/sums/pallas_call | solution.py:392
  47.4 0.6 %copy.6 = f32[8,512]{1,0:T(8,128)} copy(f32[8,512]{1,0:T(8,128)S(1)} %sums.1) | data formatting | bytes 32768
Async XLA Ops:
  0.0 1.6 %copy-start = (bf16[2,1024,512]{2,1,0:T(8,128)(2,1)S(1)}, bf16[2,1024,512]{2,1,0:T(8,128)(2,1)}, u32[]{:S(2)}) copy-start(bf16[2,1024,512]{2,1,0:T(8,128)(2,1)} %spectra_ref.1) | copy-start | bytes 6291460
  1.6 0.7 %copy-start.1 = (s32[4096]{0:T(1024)S(1)}, s32[4096]{0:T(1024)}, u32[]{:S(2)}) copy-start(s32[4096]{0:T(1024)} %param.5) | copy-start | bytes 49156
  2.3 0.7 %copy-start.2 = (s32[4096]{0:T(1024)S(1)}, s32[4096]{0:T(1024)}, u32[]{:S(2)}) copy-start(s32[4096]{0:T(1024)} %param.6) | copy-start | bytes 49156
  3.0 0.7 %copy-start.3 = (s32[4096]{0:T(1024)S(1)}, s32[4096]{0:T(1024)}, u32[]{:S(2)}) copy-start(s32[4096]{0:T(1024)} %param.7) | copy-start | bytes 49156

commit v4 on v3

--- a/solution.py
+++ b/solution.py
@@ -149,9 +149,9 @@
     shift = REACH - seg * channels
     for index_load in index_loads:
         index_load.wait()
-    first_out[...] = (index_in[0] + shift) * parts
-    second_out[...] = (index_in[1] + shift) * parts
-    bin_out[...] = index_in[2] * parts
+    first_out[...] = index_in[0] + shift
+    second_out[...] = index_in[1] + shift
+    bin_out[...] = index_in[2]
     distance = lax.broadcasted_iota(jnp.int32, (local_bins, local_bins), 0) - (
         lax.broadcasted_iota(jnp.int32, (local_bins, local_bins), 1)
     )
@@ -236,27 +236,25 @@
         base = step * BANKS
         updates = []
         for k, bank in enumerate(banks):
-            a = pl.multiple_of(first_ref[base + k], parts)
-            b = pl.multiple_of(second_ref[base + k], parts)
-            o = pl.multiple_of(bin_ref[base + k], parts)
-            first = rows[pl.ds(a, parts), :]
-            second = rows[pl.ds(b, parts), :]
+            o = bin_ref[base + k]
+            first = rows[first_ref[base + k]]
+            second = rows[second_ref[base + k]]
             turned = pltpu.roll(second, half, 0)
             real = jnp.where(upper, second, turned)
             imag = jnp.where(upper, turned, -second)
             cross = first * real + pltpu.roll(first, half, 0) * imag
-            updates.append((bank, o, bank[pl.ds(o, parts), :] + cross))
+            updates.append((bank, o, bank[o] + cross))
         for bank, o, updated in updates:
-            bank[pl.ds(o, parts), :] = updated
+            bank[o] = updated
         return carry
 
     lax.fori_loop(0, first_ref.shape[0] // BANKS, group, 0, unroll=2)
 
     lags = jnp.zeros((bins, LAGS), jnp.float32)
     for j in range(parts):
-        piece = banks[0][pl.ds(j, bins, stride=parts), :]
+        piece = banks[0][:, j, :]
         for bank in banks[1:]:
-            piece = piece + bank[pl.ds(j, bins, stride=parts), :]
+            piece = piece + bank[:, j, :]
         high = piece.astype(jnp.bfloat16)
         low = (piece - high.astype(jnp.float32)).astype(jnp.bfloat16)
         basis = table[j * LANES : (j + 1) * LANES, :]
@@ -378,10 +376,10 @@
         out_shape=jax.ShapeDtypeStruct((bins, LAGS), jnp.float32),
         in_specs=[smem, smem, smem, vmem, vmem],
         out_specs=vmem,
-        scratch_shapes=[pltpu.VMEM((bins * parts, LANES), jnp.float32)] * BANKS,
+        scratch_shapes=[pltpu.VMEM((bins, parts, LANES), jnp.float32)] * BANKS,
         compiler_params=pltpu.CompilerParams(vmem_limit_bytes=32 * 2**20),
         name="pairs",
-    )(*indices, rows, table)
+    )(*indices, rows.reshape(-1, parts, LANES), table)
 
 
 def sum_lags(lags, segments, bands):

time: 48.4 us -> 53.1 us (1.097)
  Pallas kernels: 43.6 us -> 48.3 us
    pallas_call x1, Pallas kernels: 13.1 us -> 17.8 us  [stack_pairs(): pl.pallas_call(functools.partial(pair_kernel, local_bins, bins), out_shap...]
where the time goes in v4:
time: 53.1 us; the launch traced here: 52.7 us
  Pallas kernels  48.3 us (91%)
  local copies, waits for them, and re-layouts  4.35 us (8%)
    pallas_call x1, Pallas kernels, sum_lags(): pl.pallas_call(functools.partial(sum_kernel, segments, bands), out_shape=...  20.3 us
    pallas_call x1, Pallas kernels, stack_pairs(): pl.pallas_call(functools.partial(pair_kernel, local_bins, bins), out_shap...  17.8 us
    pallas_call x1, Pallas kernels, whiten(): pl.pallas_call(functools.partial(whiten_kernel, segments, bands), out_sha...  10.3 us
    unnamed x9, local copies, waits for them, and re-layouts  4.35 us

profile of v4, /device:TPU:0, one launch (start us, length us, event | category | flops | bytes accessed | tf_op | source)
XLA Modules:
  0.0 52.7 jit_solution(2306955945064823946)
XLA Ops:
  0.0 0.0 copy-start
  0.0 1.6 %copy-done = bf16[2,1024,512]{2,1,0:T(8,128)(2,1)S(1)} copy-done((bf16[2,1024,512]{2,1,0:T(8,128)(2,1)S(1)}, bf16[2,1024,512]{2,1,0:T(8,128)(2,1)}, u32[]{:S(2)}) %copy-start) | copy-done | bytes 2097176
  1.6 0.0 copy-start.1
  1.6 0.7 %copy-done.1 = s32[4096]{0:T(1024)S(1)} copy-done((s32[4096]{0:T(1024)S(1)}, s32[4096]{0:T(1024)}, u32[]{:S(2)}) %copy-start.1) | copy-done | bytes 16408
  2.3 0.0 copy-start.2
  2.3 0.7 %copy-done.2 = s32[4096]{0:T(1024)S(1)} copy-done((s32[4096]{0:T(1024)S(1)}, s32[4096]{0:T(1024)}, u32[]{:S(2)}) %copy-start.2) | copy-done | bytes 16408
  3.0 0.0 copy-start.3
  3.0 0.7 %copy-done.3 = s32[4096]{0:T(1024)S(1)} copy-done((s32[4096]{0:T(1024)S(1)}, s32[4096]{0:T(1024)}, u32[]{:S(2)}) %copy-start.3) | copy-done | bytes 16408
  3.7 10.3 %whiten.1 = (f32[12288,128]{1,0:T(8,128)S(1)}, bf16[1024,1024]{1,0:T(8,128)(2,1)S(1)}, s32[32,128]{1,0:T(8,128)S(1)}, s32[32,128]{1,0:T(8,128)S(1)}, s32[32,128]{1,0:T(8,128)S(1)}) custom-call(bf16[2,1024,512]{2,1,0:T(8,128)(2,1)S(1)} %copy-done, s32[32,128]{1,0:T(8,128)S(1)} %bitcast.8, s32[32,128]{1,0:T(8,128)S(1)} %bitcast.9, s32[32,128]{1,0:T(8,128)S(1)} %bitcast.10), custom_call_target="tpu_custom_call" | custom-call | tf_op jit(solution)/shard_map/whiten/pallas_call | solution.py:344
  14.0 17.8 %pairs.1.lags_ref = f32[128,1024]{1,0:T(8,128)S(1)} custom-call(s32[4096]{0:T(1024)S(1)} %bitcast.11, s32[4096]{0:T(1024)S(1)} %bitcast.12, s32[4096]{0:T(1024)S(1)} %bitcast.13, f32[1536,8,128]{2,1,0:T(8,128)S(1)} %bitcast.7, bf16[1024,1024]{1,0:T(8,128)(2,1)S(1)} %get-tuple-element.14.table), custom_call_target="tpu_custom_call" | custom-call | tf_op jit(solution)/shard_map/pairs/pallas_call | solution.py:374
  31.8 20.3 %sums.1 = f32[8,512]{1,0:T(8,128)S(1)} custom-call(f32[128,1024]{1,0:T(8,128)S(1)} %pairs.1.lags_ref), custom_call_target="tpu_custom_call" | custom-call | tf_op jit(solution)/shard_map/sums/pallas_call | solution.py:390
  52.1 0.6 %copy.6 = f32[8,512]{1,0:T(8,128)} copy(f32[8,512]{1,0:T(8,128)S(1)} %sums.1) | data formatting | bytes 32768
Async XLA Ops:
  0.0 1.6 %copy-start = (bf16[2,1024,512]{2,1,0:T(8,128)(2,1)S(1)}, bf16[2,1024,512]{2,1,0:T(8,128)(2,1)}, u32[]{:S(2)}) copy-start(bf16[2,1024,512]{2,1,0:T(8,128)(2,1)} %spectra_ref.1) | copy-start | bytes 6291460
  1.6 0.7 %copy-start.1 = (s32[4096]{0:T(1024)S(1)}, s32[4096]{0:T(1024)}, u32[]{:S(2)}) copy-start(s32[4096]{0:T(1024)} %param.5) | copy-start | bytes 49156
  2.3 0.7 %copy-start.2 = (s32[4096]{0:T(1024)S(1)}, s32[4096]{0:T(1024)}, u32[]{:S(2)}) copy-start(s32[4096]{0:T(1024)} %param.6) | copy-start | bytes 49156
  3.0 0.7 %copy-start.3 = (s32[4096]{0:T(1024)S(1)}, s32[4096]{0:T(1024)}, u32[]{:S(2)}) copy-start(s32[4096]{0:T(1024)} %param.7) | copy-start | bytes 49156

commit v5 on v3

--- a/solution.py
+++ b/solution.py
@@ -13,7 +13,7 @@
 FREQ = 1024
 LAGS = 1024
 HALF_WIN = 64
-BANKS = 8
+BANKS = 4
 LANES = 128
 FINE = 32
 NEAR_SEGS = 4
@@ -250,7 +250,7 @@
             bank[pl.ds(o, parts), :] = updated
         return carry
 
-    lax.fori_loop(0, first_ref.shape[0] // BANKS, group, 0, unroll=2)
+    lax.fori_loop(0, first_ref.shape[0] // BANKS, group, 0, unroll=4)
 
     lags = jnp.zeros((bins, LAGS), jnp.float32)
     for j in range(parts):

time: 48.4 us -> 47.8 us (0.988)
  Pallas kernels: 43.6 us -> 43 us
    pallas_call x1, Pallas kernels: 13.1 us -> 12.4 us  [stack_pairs(): pl.pallas_call(functools.partial(pair_kernel, local_bins, bins), out_shap...]
where the time goes in v5:
time: 47.8 us; the launch traced here: 47.4 us
  Pallas kernels  43 us (90%)
  local copies, waits for them, and re-layouts  4.35 us (9%)
    pallas_call x1, Pallas kernels, sum_lags(): pl.pallas_call(functools.partial(sum_kernel, segments, bands), out_shape=...  20.3 us
    pallas_call x1, Pallas kernels, stack_pairs(): pl.pallas_call(functools.partial(pair_kernel, local_bins, bins), out_shap...  12.4 us
    pallas_call x1, Pallas kernels, whiten(): pl.pallas_call(functools.partial(whiten_kernel, segments, bands), out_sha...  10.3 us
    unnamed x9, local copies, waits for them, and re-layouts  4.35 us

profile of v5, /device:TPU:0, one launch (start us, length us, event | category | flops | bytes accessed | tf_op | source)
XLA Modules:
  0.0 47.4 jit_solution(3154116359598763083)
XLA Ops:
  0.0 0.0 copy-start
  0.0 1.6 %copy-done = bf16[2,1024,512]{2,1,0:T(8,128)(2,1)S(1)} copy-done((bf16[2,1024,512]{2,1,0:T(8,128)(2,1)S(1)}, bf16[2,1024,512]{2,1,0:T(8,128)(2,1)}, u32[]{:S(2)}) %copy-start) | copy-done | bytes 2097176
  1.6 0.0 copy-start.1
  1.6 0.7 %copy-done.1 = s32[4096]{0:T(1024)S(1)} copy-done((s32[4096]{0:T(1024)S(1)}, s32[4096]{0:T(1024)}, u32[]{:S(2)}) %copy-start.1) | copy-done | bytes 16408
  2.3 0.0 copy-start.2
  2.3 0.7 %copy-done.2 = s32[4096]{0:T(1024)S(1)} copy-done((s32[4096]{0:T(1024)S(1)}, s32[4096]{0:T(1024)}, u32[]{:S(2)}) %copy-start.2) | copy-done | bytes 16408
  3.0 0.0 copy-start.3
  3.0 0.7 %copy-done.3 = s32[4096]{0:T(1024)S(1)} copy-done((s32[4096]{0:T(1024)S(1)}, s32[4096]{0:T(1024)}, u32[]{:S(2)}) %copy-start.3) | copy-done | bytes 16408
  3.7 10.3 %whiten.1 = (f32[12288,128]{1,0:T(8,128)S(1)}, bf16[1024,1024]{1,0:T(8,128)(2,1)S(1)}, s32[32,128]{1,0:T(8,128)S(1)}, s32[32,128]{1,0:T(8,128)S(1)}, s32[32,128]{1,0:T(8,128)S(1)}) custom-call(bf16[2,1024,512]{2,1,0:T(8,128)(2,1)S(1)} %copy-done, s32[32,128]{1,0:T(8,128)S(1)} %bitcast.6, s32[32,128]{1,0:T(8,128)S(1)} %bitcast.7, s32[32,128]{1,0:T(8,128)S(1)} %bitcast.8), custom_call_target="tpu_custom_call" | custom-call | tf_op jit(solution)/shard_map/whiten/pallas_call | solution.py:346
  14.0 12.4 %pairs.1.lags_ref = f32[128,1024]{1,0:T(8,128)S(1)} custom-call(s32[4096]{0:T(1024)S(1)} %bitcast.9, s32[4096]{0:T(1024)S(1)} %bitcast.10, s32[4096]{0:T(1024)S(1)} %bitcast.11, f32[12288,128]{1,0:T(8,128)S(1)} %get-tuple-element.13.rows, bf16[1024,1024]{1,0:T(8,128)(2,1)S(1)} %get-tuple-element.14.table), custom_call_target="tpu_custom_call" | custom-call | tf_op jit(solution)/shard_map/pairs/pallas_call | solution.py:376
  26.4 20.3 %sums.1 = f32[8,512]{1,0:T(8,128)S(1)} custom-call(f32[128,1024]{1,0:T(8,128)S(1)} %pairs.1.lags_ref), custom_call_target="tpu_custom_call" | custom-call | tf_op jit(solution)/shard_map/sums/pallas_call | solution.py:392
  46.8 0.6 %copy.6 = f32[8,512]{1,0:T(8,128)} copy(f32[8,512]{1,0:T(8,128)S(1)} %sums.1) | data formatting | bytes 32768
Async XLA Ops:
  0.0 1.6 %copy-start = (bf16[2,1024,512]{2,1,0:T(8,128)(2,1)S(1)}, bf16[2,1024,512]{2,1,0:T(8,128)(2,1)}, u32[]{:S(2)}) copy-start(bf16[2,1024,512]{2,1,0:T(8,128)(2,1)} %spectra_ref.1) | copy-start | bytes 6291460
  1.6 0.7 %copy-start.1 = (s32[4096]{0:T(1024)S(1)}, s32[4096]{0:T(1024)}, u32[]{:S(2)}) copy-start(s32[4096]{0:T(1024)} %param.5) | copy-start | bytes 49156
  2.3 0.7 %copy-start.2 = (s32[4096]{0:T(1024)S(1)}, s32[4096]{0:T(1024)}, u32[]{:S(2)}) copy-start(s32[4096]{0:T(1024)} %param.6) | copy-start | bytes 49156
  3.0 0.7 %copy-start.3 = (s32[4096]{0:T(1024)S(1)}, s32[4096]{0:T(1024)}, u32[]{:S(2)}) copy-start(s32[4096]{0:T(1024)} %param.7) | copy-start | bytes 49156
